TPU v7x, 512 devices: a whole 4x8x8 slice. The times are simulated.
512 devices in a mesh: var: 64 (over y, x, z_lo), head: 8 (over z_hi, core).
Axes of the slice: x: 4, y: 8, z: 8 (z_hi: 4, z_lo: 2; z = z_hi * 2 + z_lo), core: 2. Of those that a mesh axis runs over, the one named last changes fastest.
Arguments:
- series: float32 [8192, 8192], P('var', 'head'), may hold values from -48 to 48
- emb_weight: float32 [8192, 512], P('head'), as said below
- emb_bias: float32 [512], replicated, may hold values from -3 to 3
- q_weight: float32 [512, 512], P(None, 'head'), may hold values from -0.75 to 0.75
- k_weight: float32 [512, 512], P(None, 'head'), may hold values from -0.25 to 0.25
- v_weight: float32 [512, 512], P(None, 'head'), may hold values from -0.25 to 0.25
- out_weight: float32 [512, 512], P('head'), may hold values from -0.25 to 0.25
- norm1_gain: float32 [512], replicated, may hold values from 0.1 to 1.9
- norm1_bias: float32 [512], replicated, may hold values from -3 to 3
- ffn_in: float32 [512, 2048], P(None, 'head'), may hold values from -0.25 to 0.25
- ffn_out: float32 [2048, 512], P('head'), may hold values from -0.1875 to 0.1875
- norm2_gain: float32 [512], replicated, may hold values from 0.1 to 1.9
- norm2_bias: float32 [512], replicated, may hold values from -3 to 3
Outputs:
- final: float32 [512, 8192], P('head', 'var')
Inputs may be any that keep to these rules, and one draw needn't show every extreme that they name: `emb_weight`: every entry lies within 12 / sqrt(8192) in magnitude, and some entry reaches that bound.
All inputs are finite; a program needn't handle non-finite values.
Results may differ from a plain program's by a relative error of at most 0.0003.
Values sent between devices are 32-bit elements; how exact they have to be, the bound alone decides.
A program may use at most 64 MiB of HBM per device.

v0:
```python
import math

import jax
import jax.numpy as jnp
from jax import lax
from jax.sharding import PartitionSpec as P

DH = 64


HIGH = lax.Precision.HIGHEST


def product(first_op, second_op):
    return jnp.dot(first_op, second_op, precision=HIGH, preferred_element_type=jnp.float32)


def project_cols(weight, stream):
    return lax.dot_general(
        weight, stream, (((0,), (1,)), ((), ())), precision=HIGH, preferred_element_type=jnp.float32
    )


def layer_norm(stream, scale_gain, shift_bias):
    centre = jnp.mean(stream, axis=-1, keepdims=True)
    spread = stream - centre
    variance = jnp.mean(spread * spread, axis=-1, keepdims=True)
    return spread * lax.rsqrt(variance + 1e-05) * scale_gain + shift_bias


def fold_keys(state, pieces, queries, local_heads):
    key_piece, value_piece = pieces
    piece_len = key_piece.shape[1]
    block_count = max(1, piece_len // 1024)
    while piece_len % block_count:
        block_count += 1
    block_len = piece_len // block_count
    score_scale = 1.0 / math.sqrt(DH)

    def advance(block_num, carry):
        run_max, run_sum, run_acc = carry
        key_block = lax.dynamic_slice_in_dim(
            key_piece, block_num * block_len, block_len, 1
        ).reshape(local_heads, DH, block_len)
        value_block = lax.dynamic_slice_in_dim(
            value_piece, block_num * block_len, block_len, 1
        ).reshape(local_heads, DH, block_len)
        scores = (
            jnp.einsum(
                "hdk,hdq->hkq",
                key_block,
                queries,
                precision=HIGH,
                preferred_element_type=jnp.float32,
            )
            * score_scale
        )
        new_max = jnp.maximum(run_max, jnp.max(scores, axis=1))
        weights = jnp.exp(scores - new_max[:, None, :])
        rescale = jnp.exp(run_max - new_max)
        new_sum = run_sum * rescale + jnp.sum(weights, axis=1)
        new_acc = run_acc * rescale[:, None, :] + jnp.einsum(
            "hdk,hkq->hdq", value_block, weights, precision=HIGH, preferred_element_type=jnp.float32
        )
        return (new_max, new_sum, new_acc)

    return lax.fori_loop(0, block_count, advance, state)


def on_device(
    series,
    emb_weight,
    emb_bias,
    q_weight,
    k_weight,
    v_weight,
    out_weight,
    norm1_gain,
    norm1_bias,
    ffn_in,
    ffn_out,
    norm2_gain,
    norm2_bias,
):
    head_count = lax.axis_size("head")
    head_pos = lax.axis_index("head")
    model_width = emb_bias.shape[0]
    col_count = model_width // head_count
    col_start = head_pos * col_count
    partial_emb = product(series, emb_weight)
    embedded = lax.psum(partial_emb, "head") + emb_bias
    query_count = embedded.shape[0]
    local_heads = q_weight.shape[1] // DH
    queries = project_cols(q_weight, embedded).reshape(local_heads, DH, query_count)
    key_t = project_cols(k_weight, embedded)
    value_t = project_cols(v_weight, embedded)
    start_state = (
        jnp.full((local_heads, query_count), -1e30, jnp.float32),
        jnp.zeros((local_heads, query_count), jnp.float32),
        jnp.zeros((local_heads, DH, query_count), jnp.float32),
    )
    state = fold_keys(
        start_state,
        (
            lax.all_gather(key_t, "var", axis=1, tiled=True),
            lax.all_gather(value_t, "var", axis=1, tiled=True),
        ),
        queries,
        local_heads,
    )
    run_max, run_sum, run_acc = state
    mixed_t = (run_acc / run_sum[:, None, :]).reshape(local_heads * DH, query_count)
    partial_out = lax.dot_general(
        mixed_t,
        out_weight,
        (((0,), (0,)), ((), ())),
        precision=HIGH,
        preferred_element_type=jnp.float32,
    )
    attention = lax.psum(partial_out, "head")
    normed = layer_norm(embedded + attention, norm1_gain, norm1_bias)
    hidden = jax.nn.gelu(product(normed, ffn_in), approximate=False)
    ffn_t = lax.psum_scatter(
        lax.dot_general(
            ffn_out,
            hidden,
            (((0,), (1,)), ((), ())),
            precision=HIGH,
            preferred_element_type=jnp.float32,
        ),
        "head",
        scatter_dimension=0,
        tiled=True,
    )
    resid_t = lax.dynamic_slice_in_dim(normed, col_start, col_count, 1).T + ffn_t
    col_sums = lax.psum((jnp.sum(resid_t, axis=0), jnp.sum(resid_t * resid_t, axis=0)), "head")
    centre = col_sums[0] / model_width
    variance = col_sums[1] / model_width - centre * centre
    gain_part = lax.dynamic_slice_in_dim(norm2_gain, col_start, col_count)
    bias_part = lax.dynamic_slice_in_dim(norm2_bias, col_start, col_count)
    return (resid_t - centre[None, :]) * lax.rsqrt(variance[None, :] + 1e-05) * gain_part[
        :, None
    ] + bias_part[:, None]


def solution(mesh):
    return jax.shard_map(
        on_device,
        mesh=mesh,
        in_specs=(
            P("var", "head"),
            P("head", None),
            P(),
            P(None, "head"),
            P(None, "head"),
            P(None, "head"),
            P("head", None),
            P(),
            P(),
            P(None, "head"),
            P("head", None),
            P(),
            P(),
        ),
        out_specs=P("head", "var"),
        check_vma=False,
    )
```

profile of v0, /device:TPU:1, one launch (start us, length us, event | category | flops | bytes accessed | tf_op | source)
XLA Modules:
  0.0 740.2 jit_solution(6087826763775134267)
XLA Ops:
  6.6 1.5 copy-done
  8.1 3.0 fusion.142
  11.2 83.3 %all-reduce.4.cloned.1.call-done = f32[128,512]{1,0:T(8,128)} async-done(((f32[128,512]{1,0:T(8,128)}), f32[128,512]{1,0:T(8,128)}) %all-reduce.4.cloned.1.call-update) | async-done | bytes 262160 | tf_op jit(solution)/shard_map/psum | solution.py:91
  94.6 2.0 convolution_bitcast_fusion.4
  96.6 1.9 convolution_bitcast_fusion.2
  98.7 1.3 convolution_bitcast_fusion.3
  100.0 199.2 %all-gather.3.cloned.1.call-done = f32[64,8192]{1,0:T(8,128)} async-done(((f32[64,128]{1,0:T(8,128)}), f32[64,8192]{1,0:T(8,128)}) %all-gather.3.cloned.1.call-update) | async-done | bytes 2097168 | tf_op jit(solution)/shard_map/all_gather | solution.py:105
  299.2 236.4 %all-gather.5.cloned.1.call-done = f32[64,8192]{1,0:T(8,128)} async-done(((f32[64,128]{1,0:T(8,128)}), f32[64,8192]{1,0:T(8,128)}) %all-gather.5.cloned.1.call-update) | async-done | bytes 2097168 | tf_op jit(solution)/shard_map/all_gather | solution.py:106
  535.6 29.2 %while.18 = (s32[]{:T(128)}, f32[1,128]{1,0:T(1,128)S(1)}, f32[1,128]{1,0:T(1,128)S(1)}, f32[1,64,128]{2,1,0:T(8,128)S(1)}, f32[64,8192]{1,0:T(8,128)}, /*index=...) while((s32[]{:T(128)}, f32[1,128]{1,0:T(1,128)S(1)}, ...), condition=%wide.region_4.0_spmd.clone, body=%wide.region_1.0_spmd.clone.sunk | while | flops 202007296 | bytes 2203823 | solution.py:67
  535.6 2.0 fusion.160
  537.7 1.5 fusion.164
  539.3 2.0 fusion.160
  541.3 1.5 fusion.164
  543.0 2.0 fusion.160
  545.0 1.5 fusion.164
  546.6 2.0 fusion.160
  548.6 1.5 fusion.164
  550.3 2.0 fusion.160
  552.3 1.5 fusion.164
  553.9 2.0 fusion.160
  555.9 1.5 fusion.164
  557.6 2.0 fusion.160
  559.6 1.5 fusion.164
  561.2 2.0 fusion.160
  563.2 1.5 fusion.164
  564.9 1.1 fusion.105
  566.1 108.5 %all-reduce.6.cloned.1.call-done = f32[128,512]{1,0:T(8,128)} async-done(((f32[128,512]{1,0:T(8,128)}), f32[128,512]{1,0:T(8,128)}) %all-reduce.6.cloned.1.call-update) | async-done | bytes 262160 | tf_op jit(solution)/shard_map/psum | solution.py:120
  674.6 1.1 fusion.140
  677.2 0.8 copy.16
  679.6 35.9 %reduce-scatter.4.cloned.1.call-done = f32[64,128]{1,0:T(8,128)} async-done(((f32[512,128]{1,0:T(8,128)}), f32[64,128]{1,0:T(8,128)}) %reduce-scatter.4.cloned.1.call-update) | async-done | bytes 32784
  715.5 0.8 copy.17
  716.6 16.3 %all-reduce = (f32[128]{0:T(128)S(1)}, f32[128]{0:T(128)S(1)}) all-reduce(f32[128]{0:T(128)S(1)} %get-tuple-element.157, f32[128]{0:T(128)S(1)} %get-tuple-element.156), channel_id=1, replica_groups=mesh['var'=64,'head'=8] {'head'}, use_global_device_ids=true, to_apply=%region_12.0 | all-reduce | flops 256 | bytes 2048 | tf_op jit(solution)/shard_map/psum | solution.py:136
  (78 shorter events, 5.8 us)
Async XLA Ops:
  6.5 1.6 copy-start
  6.5 88.0 %copy-start.7 = (f32[512]{0:T(512)S(1)}, f32[512]{0:T(512)}, u32[]{:S(2)}) copy-start(f32[512]{0:T(512)} %param.17) | copy-start | bytes 6148
  6.5 88.0 %copy-start.3 = (f32[512,64]{0,1:T(8,128)S(1)}, f32[512,64]{0,1:T(8,128)}, u32[]{:S(2)}) copy-start(f32[512,64]{0,1:T(8,128)} %param.19) | copy-start | bytes 393220
  6.5 90.1 %copy-start.4 = (f32[512,64]{0,1:T(8,128)S(1)}, f32[512,64]{0,1:T(8,128)}, u32[]{:S(2)}) copy-start(f32[512,64]{0,1:T(8,128)} %param.20) | copy-start | bytes 393220
  6.5 92.1 %copy-start.5 = (f32[512,64]{0,1:T(8,128)S(1)}, f32[512,64]{0,1:T(8,128)}, u32[]{:S(2)}) copy-start(f32[512,64]{0,1:T(8,128)} %param.18) | copy-start | bytes 393220
  6.5 88.0 %all-reduce.4.cloned.1.call-start = ((), (), s32[]{:S(2)}) async-start(), calls=%async_computation.1 | async-start | bytes 524288 | tf_op jit(solution)/shard_map/psum | solution.py:91
  11.2 288.0 %all-gather.3.cloned.1.call-start = ((), (), s32[]{:S(2)}) async-start(), calls=%async_computation.2 | async-start | bytes 2129920 | tf_op jit(solution)/shard_map/all_gather | solution.py:105
  96.5 439.1 %all-gather.5.cloned.1.call-start = ((), (), s32[]{:S(2)}) async-start(), calls=%async_computation.3 | async-start | bytes 2129920 | tf_op jit(solution)/shard_map/all_gather | solution.py:106
  98.6 576.0 %all-reduce.6.cloned.1.call-start = ((), (), s32[]{:S(2)}) async-start(), calls=%async_computation.4 | async-start | bytes 524288 | tf_op jit(solution)/shard_map/psum | solution.py:120
  535.6 29.3 %copy-start.6 = (f32[64,512]{1,0:T(8,128)S(1)}, f32[64,512]{1,0:T(8,128)}, u32[]{:S(2)}) copy-start(f32[64,512]{1,0:T(8,128)} %param.21) | copy-start | bytes 393220
  535.6 139.0 %copy-start.1 = (f32[128,512]{1,0:T(8,128)S(1)}, f32[128,512]{1,0:T(8,128)}, u32[]{:S(2)}) copy-start(f32[128,512]{1,0:T(8,128)} %all-reduce.4.cloned.1.call-done) | copy-start | bytes 786436
  535.6 140.3 %copy-start.8 = (f32[512]{0:T(512)S(1)}, f32[512]{0:T(512)}, u32[]{:S(2)}) copy-start(f32[512]{0:T(512)} %param.23) | copy-start | bytes 6148
  535.6 140.3 %copy-start.9 = (f32[512]{0:T(512)S(1)}, f32[512]{0:T(512)}, u32[]{:S(2)}) copy-start(f32[512]{0:T(512)} %param.22) | copy-start | bytes 6148
  564.9 111.2 %copy-start.2 = (f32[512,256]{1,0:T(8,128)S(1)}, f32[512,256]{1,0:T(8,128)}, u32[]{:S(2)}) copy-start(f32[512,256]{1,0:T(8,128)} %param.24) | copy-start | bytes 1572868
  566.0 149.5 %reduce-scatter.4.cloned.1.call-start = ((), (), s32[]{:S(2)}) async-start(), calls=%async_computation.5 | async-start | bytes 294912
  674.6 1.9 copy-start.10
Sparse Core Ops, SparseCore 0:
  11.3 83.2 all-reduce.3
  96.8 202.3 all-gather.2
  301.4 234.1 all-gather.4
  566.1 108.3 all-reduce.5
  678.2 37.2 reduce-scatter.3
where the time goes:
time: 741 us; the launch traced here: 740 us
  waiting for transfers between devices  663 us (89%)
  matrix products  38 us (5%)
  blocking collectives  16.3 us (2%)
  between operations  13.3 us (2%)
    all_gather x1, waiting for transfers between devices, on_device(): lax.all_gather(value_t, 'var', axis=1, tiled=True)  236 us
    all_gather x1, waiting for transfers between devices, on_device(): lax.all_gather(key_t, 'var', axis=1, tiled=True)  199 us
    psum x1, waiting for transfers between devices, on_device(): attention = lax.psum(partial_out, 'head')  109 us
    psum x1, waiting for transfers between devices, on_device(): embedded = lax.psum(partial_emb, 'head') + emb_bias  83.3 us
    unnamed x6, waiting for transfers between devices  36 us
    psum x1, blocking collectives, on_device(): lax.psum((jnp.sum(resid_t, axis=0), jnp.sum(resid_t * resid_t, axis=0)),...  16.3 us
    dot_general x8, matrix products, advance(): jnp.einsum('hdk,hdq->hkq', key_block, queries, precision=HIGH, preferred_...  15.8 us
  transfers between devices with their start and end apart: 5, of which 5 were waited for; matrix products, arithmetic and copies ran while one was open for 1% of the time, Pallas kernels for 0%

commit v1 on v0

v1 whole, which is shorter than its diff:
```python
import functools
import math

import jax
import jax.numpy as jnp
from jax import lax
from jax.experimental import pallas as pl
from jax.experimental.pallas import tpu as pltpu
from jax.sharding import PartitionSpec as P

MESH = pl.DeviceIdType.MESH
F32 = jnp.float32
BF16 = jnp.bfloat16

D = 512
FF_PART = 256
DH = 64
ROWS = 128
NY, NX, NZL, NZH, NC = 8, 4, 2, 4, 2
NHEAD = NZH * NC
Z_OFFS = (2, 1, 3)
Y_ORDER = (4, 3, 5, 2, 6, 1, 7, 0)
KV_OFFS = ((2, 1), (2, 0), (1, 1), (3, 1), (1, 0), (3, 0), (0, 1))
COPIES = 96
EPS = 1e-05


def halves(x):
    top = x.astype(BF16)
    return top, (x - top.astype(F32)).astype(BF16)


def mxu(a, b):
    return lax.dot_general(a, b, (((1,), (0,)), ((), ())), preferred_element_type=F32)


def quads(r, m, n):
    return r[:m, :n] + ((r[:m, n:] + r[m:, :n]) + r[m:, n:])


def side_by_side(x):
    return jnp.concatenate(halves(x), axis=1)


def stacked(x):
    return jnp.concatenate(halves(x), axis=0)


def column(row):
    return jnp.broadcast_to(row, (128, 128)).T


def layer_kernel(
    series_h, ew_h, eb_h, qw_h, kw_h, vw_h, ow_h, n1g_h, n1b_h, fi_h, fo_h, n2g_h, n2b_h,
    out_ref,
    series, ew, qw, kw, vw, ow, fi, fo, vec,
    wqkv, fit, fot, wot, gath, n1g, n1b, own_vec,
    epart, cbuf, sbuf, rsbuf, efull,
    qsend, ksend, vsend, qbuf, kbuf, vbuf, kst, qst, vst,
    osend, obuf, mfull, normed_ref,
    fpart, fcbuf, fsbuf, frsbuf, stat, statbuf,
    lsem, ssem, rsem,
):
    v = lax.axis_index("var")
    h = lax.axis_index("head")
    y, x, zl = v // (NX * NZL), (v // NZL) % NX, v % NZL
    zh, c = h // NC, h % NC
    oc = 1 - c

    def at(y_, x_, zl_, zh_, c_):
        return ((y_ * NX + x_) * NZL + zl_, zh_ * NC + c_)

    core_dev = at(y, x, zl, zh, oc)
    z_devs = [at(y, x, zl, (zh + off) % NZH, c) for off in Z_OFFS]
    x_devs = [at(y, (x + off) % NX, zl, zh, c) for off in (2, 1, 3)]
    head_devs = [(v, (h + off) % NHEAD) for off in range(1, NHEAD)]
    y_to = {off: at((y + off) % NY, x, zl, zh, c) for off in range(1, NY)}
    y_from = {off: at((y + NY - off) % NY, x, zl, zh, c) for off in range(1, NY)}
    kv_devs = [at(y, (x + dx) % NX, (zl + dz) % NZL, zh, c) for dx, dz in KV_OFFS]

    count = [0]
    pending = []

    def send(src, dst, dev):
        i = count[0]
        count[0] += 1
        cp = pltpu.make_async_remote_copy(
            src_ref=src, dst_ref=dst, send_sem=ssem.at[i], recv_sem=rsem.at[i],
            device_id=dev, device_id_type=MESH,
        )
        cp.start()
        pending.append(cp)
        return cp

    def drain():
        while pending:
            pending.pop(0).wait_send()

    lcount = [0]

    def load(src, dst):
        i = lcount[0]
        lcount[0] += 1
        cp = pltpu.make_async_copy(src, dst, lsem.at[i])
        cp.start()
        return cp

    ld_series = load(series_h, series)
    z_order = [(zh + off) % NZH for off in Z_OFFS] + [zh]
    ld_ew = [
        load(ew_h.at[:, pl.ds(pl.multiple_of(zz * 128, 128), 128)], ew.at[k])
        for k, zz in enumerate(z_order)
    ]
    ld_ow = load(ow_h, ow)
    ld_vec = [load(r, vec.at[i]) for i, r in enumerate((eb_h, n1g_h, n1b_h, n2g_h, n2b_h))]
    ld_qkv = [load(a, b) for a, b in ((qw_h, qw), (kw_h, kw), (vw_h, vw))]
    ld_ffn = [load(a, b) for a, b in ((fi_h, fi), (fo_h, fo))]

    barrier = pltpu.get_barrier_semaphore()
    greeted = head_devs + [y_to[off] for off in range(1, NY)] + kv_devs
    for dev in greeted:
        pl.semaphore_signal(barrier, inc=1, device_id=dev, device_id_type=MESH)

    ld_series.wait()
    s_stack = stacked(series[...])

    def emb_step(k):
        ld_ew[k].wait()
        r = mxu(s_stack, side_by_side(ew[k]))
        epart[k] = quads(r, ROWS, 128).T.reshape(NC, DH, ROWS)

    emb_step(0)
    ld_ow.wait()
    pl.semaphore_wait(barrier, len(greeted))

    core_cps = [send(epart.at[0, oc], cbuf.at[0], core_dev)]
    xrows = pl.ds(pl.multiple_of(x * 16, 16), 16)
    gath[c, x, zh] = ow[xrows, :]
    w_z = [send(gath.at[c, x, zh], gath.at[c, x, zh], dev) for dev in z_devs]
    emb_step(1)
    core_cps.append(send(epart.at[1, oc], cbuf.at[1], core_dev))
    z_cps = []

    def to_chip(k):
        core_cps[k].wait_recv()
        sbuf[k] = epart[k, c] + cbuf[k]
        if k < 3:
            z_cps.append(send(sbuf.at[k], rsbuf.at[k], z_devs[k]))

    to_chip(0)
    emb_step(2)
    core_cps.append(send(epart.at[2, oc], cbuf.at[2], core_dev))
    to_chip(1)
    emb_step(3)
    core_cps.append(send(epart.at[3, oc], cbuf.at[3], core_dev))
    to_chip(2)
    to_chip(3)

    for ld in ld_vec + ld_qkv:
        ld.wait()
    kt = kw[...].T
    wqkv[...] = stacked(jnp.concatenate([qw[...].T, vw[...].T, kt, kt], axis=0))
    for i, j in enumerate((0, 3, 4)):
        own_vec[i] = column(vec[j, pl.ds(zh, 1), :]).reshape(NC, DH, ROWS)
    for cp in w_z:
        cp.wait_recv()
    w_x = [send(gath.at[c, x], gath.at[c, x], dev) for dev in x_devs]

    for cp in z_cps:
        cp.wait_recv()
    efull[h] = (sbuf[3] + rsbuf[1]) + (rsbuf[0] + rsbuf[2]) + own_vec[0, c]

    def gather_heads(buf, meanwhile):
        zs = [send(buf.at[h], buf.at[h], dev) for dev in z_devs]
        cs = [send(buf.at[h], buf.at[h], core_dev)]
        meanwhile()
        for k in (1, 2, 0):
            zs[k].wait_recv()
            hs = ((zh + NZH - Z_OFFS[k]) % NZH) * NC + c
            cs.append(send(buf.at[hs], buf.at[hs], core_dev))
        for cp in cs:
            cp.wait_recv()

    def prepare_ffn_in():
        ld_ffn[0].wait()
        fit[...] = stacked(fi[...].T)

    gather_heads(efull, prepare_ffn_in)

    emb_t = efull[...].reshape(D, ROWS)
    qkv = quads(mxu(wqkv[...], side_by_side(emb_t)), 4 * DH, ROWS)
    qsend[...] = qkv[:DH] * (math.log2(math.e) / math.sqrt(DH))
    kk = qkv[2 * DH :].T
    left = lax.broadcasted_iota(jnp.int32, (DH, 128), 1) < DH
    ksend[...] = jnp.where(left, kk[:DH], kk[DH:])
    vsend[...] = qkv[DH : 2 * DH]

    q_cps, k_cps, v_cps = {}, [], []
    for i in range(7):
        off = Y_ORDER[i]
        k_cps.append(send(ksend, kbuf.at[i], kv_devs[i]))
        q_cps[off] = send(qsend, qbuf.at[off], y_to[off])
    for i in range(7):
        v_cps.append(send(vsend, vbuf.at[i], kv_devs[i]))

    for cp in w_x:
        cp.wait_recv()
    w_c = send(gath.at[c], gath.at[c], core_dev)
    ld_ffn[1].wait()
    for z in range(NZH):
        fot[z] = stacked(fo[:, z * 128 : (z + 1) * 128].T)
        n1g[pl.ds(z * 128, 128), :] = column(vec[1, z : z + 1, :])
        n1b[pl.ds(z * 128, 128), :] = column(vec[2, z : z + 1, :])
    w_c.wait_recv()
    for z in range(NZH):
        block = jnp.concatenate(
            [gath[par, xx, z] for par in range(NC) for xx in range(NX)], axis=0
        )
        top, rest = halves(block.T)
        wot[:D, z * 128 : (z + 1) * 128] = top
        wot[D:, z * 128 : (z + 1) * 128] = rest

    def put_key(i, pack):
        other = pltpu.roll(pack, DH, 1)
        for j, kd in enumerate((jnp.where(left, pack, other), jnp.where(left, other, pack))):
            top, rest = halves(kd)
            rows = slice(i * ROWS + j * DH, i * ROWS + (j + 1) * DH)
            kst[rows, :128] = top
            kst[rows, 128:] = rest

    def put_query(j, qt):
        top, rest = halves(qt)
        cols = slice(j * ROWS, (j + 1) * ROWS)
        for r in range(2):
            qst[2 * r * DH : (2 * r + 1) * DH, cols] = top
            qst[(2 * r + 1) * DH : (2 * r + 2) * DH, cols] = rest

    def put_value(i, vt):
        vst[:, i * ROWS : (i + 1) * ROWS] = stacked(vt)

    put_key(7, ksend[...])
    put_value(7, vsend[...])
    put_query(7, qsend[...])
    for i in range(7):
        k_cps[i].wait_recv()
        put_key(i, kbuf[i])
    for i in range(7):
        v_cps[i].wait_recv()
        put_value(i, vbuf[i])

    o_cps = {}
    for pair in range(4):
        for j in (2 * pair, 2 * pair + 1):
            off = Y_ORDER[j]
            if off:
                q_cps[off].wait_recv()
                put_query(j, qbuf[off])
        s = mxu(kst[...], qst[:, 2 * pair * ROWS : (2 * pair + 2) * ROWS])
        top_score = jnp.max(s, axis=0, keepdims=True)
        p = jnp.exp2(s - top_score)
        total = jnp.sum(p, axis=0, keepdims=True)
        p_top, p_rest = halves(p)
        o = mxu(vst[...], p_top) + mxu(vst[...], p_rest)
        o = o[:DH] + o[DH:]
        for j in (2 * pair, 2 * pair + 1):
            off = Y_ORDER[j]
            cols = slice((j % 2) * ROWS, (j % 2 + 1) * ROWS)
            osend[off, :DH] = o[:, cols]
            osend[off, DH : DH + 8] = jnp.concatenate(
                [
                    jnp.broadcast_to(top_score[:, cols], (4, ROWS)),
                    jnp.broadcast_to(total[:, cols], (4, ROWS)),
                ],
                axis=0,
            )
            if off:
                o_cps[off] = send(osend.at[off], obuf.at[off], y_from[off])

    for off in range(1, NY):
        o_cps[off].wait_recv()
    tops = [osend[0, DH : DH + 1]] + [obuf[off, DH : DH + 1] for off in range(1, NY)]
    best = functools.reduce(jnp.maximum, tops)
    scales = [jnp.exp2(t - best) for t in tops]
    denom = scales[0] * osend[0, DH + 4 : DH + 5]
    acc = scales[0] * osend[0, :DH]
    for off in range(1, NY):
        denom += scales[off] * obuf[off, DH + 4 : DH + 5]
        acc += scales[off] * obuf[off, :DH]
    mfull[h] = acc / denom

    gather_heads(mfull, lambda: None)

    mixed_t = mfull[...].reshape(D, ROWS)
    resid = emb_t + quads(mxu(wot[...], side_by_side(mixed_t)), D, ROWS)
    centre = jnp.sum(resid, axis=0, keepdims=True) * (1.0 / D)
    spread = resid - centre
    variance = jnp.sum(spread * spread, axis=0, keepdims=True) * (1.0 / D)
    normed = spread * lax.rsqrt(variance + EPS) * n1g[...] + n1b[...]
    normed_ref[...] = normed.reshape(NHEAD, DH, ROWS)
    hid = quads(mxu(fit[...], side_by_side(normed)), FF_PART, ROWS)
    hid = hid * (1.0 + lax.erf(hid * (1.0 / math.sqrt(2.0)))) * 0.5
    hid2 = side_by_side(hid)

    fcore = []
    for k in range(4):
        fpart[k] = quads(mxu(fot[z_order[k]], hid2), 128, ROWS).reshape(NC, DH, ROWS)
        fcore.append(send(fpart.at[k, oc], fcbuf.at[k], core_dev))
    fz = []
    for k in range(4):
        fcore[k].wait_recv()
        fsbuf[k] = fpart[k, c] + fcbuf[k]
        if k < 3:
            fz.append(send(fsbuf.at[k], frsbuf.at[k], z_devs[k]))
    for cp in fz:
        cp.wait_recv()
    r2 = (fsbuf[3] + frsbuf[1]) + (frsbuf[0] + frsbuf[2]) + normed_ref[h]

    mean_own = jnp.sum(r2, axis=0, keepdims=True) * (1.0 / DH)
    dev_own = r2 - mean_own
    m2_own = jnp.sum(dev_own * dev_own, axis=0, keepdims=True)
    stat[...] = jnp.concatenate(
        [jnp.broadcast_to(mean_own, (4, ROWS)), jnp.broadcast_to(m2_own, (4, ROWS))], axis=0
    )
    st = [send(stat, statbuf.at[i], dev) for i, dev in enumerate(head_devs)]
    for cp in st:
        cp.wait_recv()
    means = [mean_own] + [statbuf[i, 0:1] for i in range(7)]
    mean = functools.reduce(jnp.add, means) * (1.0 / NHEAD)
    m2 = functools.reduce(jnp.add, [m2_own] + [statbuf[i, 4:5] for i in range(7)])
    m2 += DH * functools.reduce(jnp.add, [(m - mean) * (m - mean) for m in means])
    scale = lax.rsqrt(m2 * (1.0 / D) + EPS)
    out_ref[...] = (r2 - mean) * scale * own_vec[1, c] + own_vec[2, c]
    drain()


def on_device(series, emb_weight, emb_bias, q_weight, k_weight, v_weight, out_weight,
              norm1_gain, norm1_bias, ffn_in, ffn_out, norm2_gain, norm2_bias):
    vec4 = lambda a: a.reshape(4, 128)
    vm = lambda *shape: pltpu.VMEM(shape, F32)
    vb = lambda *shape: pltpu.VMEM(shape, BF16)
    block = (DH, ROWS)
    scratch = [
        vm(ROWS, 1024), vm(4, 1024, 128), vm(D, DH), vm(D, DH), vm(D, DH), vm(DH, D),
        vm(D, FF_PART), vm(FF_PART, D), vm(5, 4, 128),
        vb(8 * DH, D), vb(2 * FF_PART, D), vb(4, 256, FF_PART), vb(2 * D, D),
        vm(NC, NX, NZH, 16, D), vm(D, ROWS), vm(D, ROWS), vm(3, NC, *block),
        vm(4, NC, *block), vm(4, *block), vm(4, *block), vm(3, *block), vm(NHEAD, *block),
        vm(*block), vm(*block), vm(*block), vm(NY, *block), vm(7, *block), vm(7, *block),
        vb(1024, 256), vb(256, 1024), vb(128, 1024),
        vm(NY, DH + 8, ROWS), vm(NY, DH + 8, ROWS), vm(NHEAD, *block), vm(NHEAD, *block),
        vm(4, NC, *block), vm(4, *block), vm(4, *block), vm(3, *block),
        vm(8, ROWS), vm(7, 8, ROWS),
        pltpu.SemaphoreType.DMA((16,)), pltpu.SemaphoreType.DMA((COPIES,)),
        pltpu.SemaphoreType.DMA((COPIES,)),
    ]
    return pl.pallas_call(
        layer_kernel,
        out_shape=jax.ShapeDtypeStruct(block, F32),
        in_specs=[pl.BlockSpec(memory_space=pl.ANY)] * 13,
        out_specs=pl.BlockSpec(memory_space=pltpu.VMEM),
        scratch_shapes=scratch,
        compiler_params=pltpu.CompilerParams(
            collective_id=0, has_side_effects=True, vmem_limit_bytes=40 * 1024 * 1024
        ),
        name="layer",
    )(series, emb_weight, vec4(emb_bias), q_weight, k_weight, v_weight, out_weight,
      vec4(norm1_gain), vec4(norm1_bias), ffn_in, ffn_out, vec4(norm2_gain), vec4(norm2_bias))


def solution(mesh):
    return jax.shard_map(
        on_device,
        mesh=mesh,
        in_specs=(
            P("var", "head"), P("head", None), P(), P(None, "head"), P(None, "head"),
            P(None, "head"), P("head", None), P(), P(), P(None, "head"), P("head", None), P(), P(),
        ),
        out_specs=P("head", "var"),
        check_vma=False,
    )
```

time: 741 us -> 84.1 us (0.11)
  waiting for transfers between devices: 663 us -> 0 us
  Pallas kernels: 0 us -> 70.9 us
  matrix products: 38 us -> 0 us
  blocking collectives: 16.3 us -> 0 us
  between operations: 13.3 us -> 0.05 us
    all_gather x2 -> x0, waiting for transfers between devices: 436 us -> none  [the longest x1 236 us: on_device(): lax.all_gather(value_t, 'var', axis=1, tiled=True)]
    psum x2 -> x0, waiting for transfers between devices: 192 us -> none  [the longest x1 109 us: on_device(): attention = lax.psum(partial_out, 'head')]
    pallas_call x0 -> x1, Pallas kernels: none -> 70.9 us  [on_device(): pl.pallas_call(layer_kernel, out_shape=jax.ShapeDtypeStruct(block, F32),...]
    dot_general x23 -> x0, matrix products: 38 us -> none  [the longest x8 15.8 us: advance(): jnp.einsum('hdk,hdq->hkq', key_block, queries, precision=HIGH, preferred_...]
    unnamed x6 -> x0, waiting for transfers between devices: 36 us -> none
    psum x1 -> x0, blocking collectives: 16.3 us -> none  [on_device(): lax.psum((jnp.sum(resid_t, axis=0), jnp.sum(resid_t * resid_t, axis=0)),...]
    unnamed x24, local copies, waits for them, and re-layouts: 3.24 us -> 12.7 us
  transfers between devices with their start and end apart: 5 -> 0, of which waited for: 5 -> 0; matrix products, arithmetic and copies ran while one was open for 1% -> 0% of each run, Pallas kernels for 0% -> 0%
where the time goes in v1:
time: 84.1 us; the launch traced here: 83.6 us
  Pallas kernels  70.9 us (84%)
  local copies, waits for them, and re-layouts  12.7 us (15%)
    pallas_call x1, Pallas kernels, on_device(): pl.pallas_call(layer_kernel, out_shape=jax.ShapeDtypeStruct(block, F32),...  70.9 us
    unnamed x24, local copies, waits for them, and re-layouts  12.7 us

profile of v1, /device:TPU:1, one launch (start us, length us, event | category | flops | bytes accessed | tf_op | source)
XLA Modules:
  0.0 83.6 jit_solution(6606157036996718672)
XLA Ops:
  0.0 1.0 %copy.14.qw_h = f32[512,64]{1,0:T(8,128)S(1)} copy(f32[512,64]{0,1:T(8,128)} %param.16) | data formatting | bytes 262144 | tf_op args[3]
  1.0 1.0 %copy.15.kw_h = f32[512,64]{1,0:T(8,128)S(1)} copy(f32[512,64]{0,1:T(8,128)} %param.17) | data formatting | bytes 262144 | tf_op args[4]
  2.1 1.0 %copy.16.vw_h = f32[512,64]{1,0:T(8,128)S(1)} copy(f32[512,64]{0,1:T(8,128)} %param.18) | data formatting | bytes 262144 | tf_op args[5]
  3.1 0.0 copy-start
  3.1 1.6 %copy-done = f32[1024,512]{1,0:T(8,128)S(1)} copy-done((f32[1024,512]{1,0:T(8,128)S(1)}, f32[1024,512]{1,0:T(8,128)}, u32[]{:S(2)}) %copy-start) | copy-done | bytes 2097176
  4.7 0.0 copy-start.1
  4.7 1.0 %copy-done.1 = f32[128,1024]{1,0:T(8,128)S(1)} copy-done((f32[128,1024]{1,0:T(8,128)S(1)}, f32[128,1024]{1,0:T(8,128)}, u32[]{:S(2)}) %copy-start.1) | copy-done | bytes 524312
  5.7 0.0 copy-start.2
  5.8 1.0 %copy-done.2 = f32[512,256]{1,0:T(8,128)S(1)} copy-done((f32[512,256]{1,0:T(8,128)S(1)}, f32[512,256]{1,0:T(8,128)}, u32[]{:S(2)}) %copy-start.2) | copy-done | bytes 524312
  6.8 0.0 copy-start.3
  6.8 1.0 %copy-done.3 = f32[256,512]{1,0:T(8,128)S(1)} copy-done((f32[256,512]{1,0:T(8,128)S(1)}, f32[256,512]{1,0:T(8,128)}, u32[]{:S(2)}) %copy-start.3) | copy-done | bytes 524312
  7.8 0.0 copy-start.4
  7.8 0.9 %copy-done.4 = f32[64,512]{1,0:T(8,128)S(1)} copy-done((f32[64,512]{1,0:T(8,128)S(1)}, f32[64,512]{1,0:T(8,128)}, u32[]{:S(2)}) %copy-start.4) | copy-done | bytes 131096
  8.7 0.0 copy-start.5
  8.7 0.7 copy-done.5
  9.4 0.0 copy-start.6
  9.4 0.7 copy-done.6
  10.1 0.0 copy-start.7
  10.1 0.7 copy-done.7
  10.8 0.0 copy-start.8
  10.8 0.7 copy-done.8
  11.5 0.0 copy-start.9
  11.5 0.7 copy-done.9
  12.1 70.9 %layer.1 = f32[64,128]{1,0:T(8,128)S(1)} custom-call(f32[128,1024]{1,0:T(8,128)S(1)} %copy-done.1, f32[1024,512]{1,0:T(8,128)S(1)} %copy-done, f32[4,128]{1,0:T(4,128)S(1)} %bitcast.5, f32[512,64]{1,0:T(8,128)S(1)} %copy.14.qw_h, f32[512,64]{1,0:T(8,128)S(1)} %copy.15.kw_h, f32[512,64]{1,0:T(8,128)S(1)} %copy.16.vw_h, f32[64,512]{1,0:T(8,128)S(1)} %copy-done.4, ...), custom_call_target="tpu_custom_call" | custom-call | tf_op jit(solution)/shard_map/layer/pallas_call | solution.py:356
  83.0 0.6 copy.18
Async XLA Ops:
  3.1 1.6 %copy-start = (f32[1024,512]{1,0:T(8,128)S(1)}, f32[1024,512]{1,0:T(8,128)}, u32[]{:S(2)}) copy-start(f32[1024,512]{1,0:T(8,128)} %ew_h.1) | copy-start | bytes 6291460
  4.7 1.0 %copy-start.1 = (f32[128,1024]{1,0:T(8,128)S(1)}, f32[128,1024]{1,0:T(8,128)}, u32[]{:S(2)}) copy-start(f32[128,1024]{1,0:T(8,128)} %series_h.1) | copy-start | bytes 1572868
  5.7 1.0 %copy-start.2 = (f32[512,256]{1,0:T(8,128)S(1)}, f32[512,256]{1,0:T(8,128)}, u32[]{:S(2)}) copy-start(f32[512,256]{1,0:T(8,128)} %fi_h.1) | copy-start | bytes 1572868
  6.8 1.0 %copy-start.3 = (f32[256,512]{1,0:T(8,128)S(1)}, f32[256,512]{1,0:T(8,128)}, u32[]{:S(2)}) copy-start(f32[256,512]{1,0:T(8,128)} %fo_h.1) | copy-start | bytes 1572868
  7.8 0.9 %copy-start.4 = (f32[64,512]{1,0:T(8,128)S(1)}, f32[64,512]{1,0:T(8,128)}, u32[]{:S(2)}) copy-start(f32[64,512]{1,0:T(8,128)} %ow_h.1) | copy-start | bytes 393220
  8.7 0.7 copy-start.5
  9.4 0.7 copy-start.6
  10.1 0.7 copy-start.7
  10.8 0.7 copy-start.8
  11.5 0.7 copy-start.9

commit v2 on v1

--- a/solution.py
+++ b/solution.py
@@ -19,8 +19,10 @@
 NY, NX, NZL, NZH, NC = 8, 4, 2, 4, 2
 NHEAD = NZH * NC
 Z_OFFS = (2, 1, 3)
-Y_ORDER = (4, 3, 5, 2, 6, 1, 7, 0)
-KV_OFFS = ((2, 1), (2, 0), (1, 1), (3, 1), (1, 0), (3, 0), (0, 1))
+Q_PAIRS = ((0, 1), (7, 2), (6, 3), (5, 4))
+KV_OFFS = ((1, 0), (3, 0), (0, 1), (1, 1), (3, 1), (2, 0), (2, 1))
+KV_SENDS = (7, 6, 4, 5, 3, 1, 2)
+Q_SENDS = (4, 3, 5, 2, 6, 7, 1)
 COPIES = 96
 EPS = 1e-05
 
@@ -56,10 +58,10 @@
     series, ew, qw, kw, vw, ow, fi, fo, vec,
     wqkv, fit, fot, wot, gath, n1g, n1b, own_vec,
     epart, cbuf, sbuf, rsbuf, efull,
-    qsend, ksend, vsend, qbuf, kbuf, vbuf, kst, qst, vst,
+    qsend, kvsend, qbuf, kvbuf, kst, qst, vst,
     osend, obuf, mfull, normed_ref,
     fpart, fcbuf, fsbuf, frsbuf, stat, statbuf,
-    lsem, ssem, rsem,
+    lsem, ssem, rsem, own_sem,
 ):
     v = lax.axis_index("var")
     h = lax.axis_index("head")
@@ -72,8 +74,11 @@
 
     core_dev = at(y, x, zl, zh, oc)
     z_devs = [at(y, x, zl, (zh + off) % NZH, c) for off in Z_OFFS]
+    sum_offs = (2, 1 + 2 * zl, 0, 3 - 2 * zl)
+    z_order = [(zh + off) % NZH for off in sum_offs]
+    sum_devs = [at(y, x, 1 - zl, zz, c) for zz in z_order]
     x_devs = [at(y, (x + off) % NX, zl, zh, c) for off in (2, 1, 3)]
-    head_devs = [(v, (h + off) % NHEAD) for off in range(1, NHEAD)]
+    head_devs = [(v, (h + off) % NHEAD) for off in (4, 3, 5, 2, 6, 7, 1)]
     y_to = {off: at((y + off) % NY, x, zl, zh, c) for off in range(1, NY)}
     y_from = {off: at((y + NY - off) % NY, x, zl, zh, c) for off in range(1, NY)}
     kv_devs = [at(y, (x + dx) % NX, (zl + dz) % NZL, zh, c) for dx, dz in KV_OFFS]
@@ -96,6 +101,10 @@
         while pending:
             pending.pop(0).wait_send()
 
+    def fence():
+        pl.semaphore_signal(own_sem, 1)
+        pl.semaphore_wait(own_sem, 1)
+
     lcount = [0]
 
     def load(src, dst):
@@ -106,21 +115,19 @@
         return cp
 
     ld_series = load(series_h, series)
-    z_order = [(zh + off) % NZH for off in Z_OFFS] + [zh]
     ld_ew = [
         load(ew_h.at[:, pl.ds(pl.multiple_of(zz * 128, 128), 128)], ew.at[k])
         for k, zz in enumerate(z_order)
     ]
+    barrier = pltpu.get_barrier_semaphore()
+    greeted = head_devs + sum_devs[:2] + sum_devs[3:] + [y_to[off] for off in range(1, NY)] + kv_devs
+    for dev in greeted:
+        pl.semaphore_signal(barrier, inc=1, device_id=dev, device_id_type=MESH)
     ld_ow = load(ow_h, ow)
     ld_vec = [load(r, vec.at[i]) for i, r in enumerate((eb_h, n1g_h, n1b_h, n2g_h, n2b_h))]
     ld_qkv = [load(a, b) for a, b in ((qw_h, qw), (kw_h, kw), (vw_h, vw))]
     ld_ffn = [load(a, b) for a, b in ((fi_h, fi), (fo_h, fo))]
 
-    barrier = pltpu.get_barrier_semaphore()
-    greeted = head_devs + [y_to[off] for off in range(1, NY)] + kv_devs
-    for dev in greeted:
-        pl.semaphore_signal(barrier, inc=1, device_id=dev, device_id_type=MESH)
-
     ld_series.wait()
     s_stack = stacked(series[...])
 
@@ -134,45 +141,48 @@
     pl.semaphore_wait(barrier, len(greeted))
 
     core_cps = [send(epart.at[0, oc], cbuf.at[0], core_dev)]
+    fence()
+    emb_step(1)
+    core_cps.append(send(epart.at[1, oc], cbuf.at[1], core_dev))
+    fence()
+    z_cps = []
+
+    def to_chip(k):
+        core_cps[k].wait_recv()
+        sbuf[k] = epart[k, c] + cbuf[k]
+        z_cps.append(send(sbuf.at[k], rsbuf.at[k], sum_devs[k]))
+
+    to_chip(0)
+    emb_step(2)
+    core_cps.append(send(epart.at[2, oc], cbuf.at[2], core_dev))
+    fence()
+    to_chip(1)
+    emb_step(3)
+    core_cps.append(send(epart.at[3, oc], cbuf.at[3], core_dev))
+    fence()
+    to_chip(2)
+    to_chip(3)
+
     xrows = pl.ds(pl.multiple_of(x * 16, 16), 16)
     gath[c, x, zh] = ow[xrows, :]
     w_z = [send(gath.at[c, x, zh], gath.at[c, x, zh], dev) for dev in z_devs]
-    emb_step(1)
-    core_cps.append(send(epart.at[1, oc], cbuf.at[1], core_dev))
-    z_cps = []
-
-    def to_chip(k):
-        core_cps[k].wait_recv()
-        sbuf[k] = epart[k, c] + cbuf[k]
-        if k < 3:
-            z_cps.append(send(sbuf.at[k], rsbuf.at[k], z_devs[k]))
-
-    to_chip(0)
-    emb_step(2)
-    core_cps.append(send(epart.at[2, oc], cbuf.at[2], core_dev))
-    to_chip(1)
-    emb_step(3)
-    core_cps.append(send(epart.at[3, oc], cbuf.at[3], core_dev))
-    to_chip(2)
-    to_chip(3)
+    fence()
 
     for ld in ld_vec + ld_qkv:
         ld.wait()
-    kt = kw[...].T
-    wqkv[...] = stacked(jnp.concatenate([qw[...].T, vw[...].T, kt, kt], axis=0))
+    kt = kw[...]
+    wqkv[...] = stacked(jnp.concatenate([qw[...], vw[...], kt, kt], axis=0))
     for i, j in enumerate((0, 3, 4)):
         own_vec[i] = column(vec[j, pl.ds(zh, 1), :]).reshape(NC, DH, ROWS)
-    for cp in w_z:
-        cp.wait_recv()
-    w_x = [send(gath.at[c, x], gath.at[c, x], dev) for dev in x_devs]
 
     for cp in z_cps:
         cp.wait_recv()
-    efull[h] = (sbuf[3] + rsbuf[1]) + (rsbuf[0] + rsbuf[2]) + own_vec[0, c]
+    efull[h] = (rsbuf[0] + rsbuf[1]) + (rsbuf[2] + rsbuf[3]) + own_vec[0, c]
 
     def gather_heads(buf, meanwhile):
         zs = [send(buf.at[h], buf.at[h], dev) for dev in z_devs]
         cs = [send(buf.at[h], buf.at[h], core_dev)]
+        fence()
         meanwhile()
         for k in (1, 2, 0):
             zs[k].wait_recv()
@@ -181,7 +191,12 @@
         for cp in cs:
             cp.wait_recv()
 
+    w_x = []
+
     def prepare_ffn_in():
+        for cp in w_z:
+            cp.wait_recv()
+        w_x.extend(send(gath.at[c, x], gath.at[c, x], dev) for dev in x_devs)
         ld_ffn[0].wait()
         fit[...] = stacked(fi[...].T)
 
@@ -192,16 +207,23 @@
     qsend[...] = qkv[:DH] * (math.log2(math.e) / math.sqrt(DH))
     kk = qkv[2 * DH :].T
     left = lax.broadcasted_iota(jnp.int32, (DH, 128), 1) < DH
-    ksend[...] = jnp.where(left, kk[:DH], kk[DH:])
-    vsend[...] = qkv[DH : 2 * DH]
-
-    q_cps, k_cps, v_cps = {}, [], []
-    for i in range(7):
-        off = Y_ORDER[i]
-        k_cps.append(send(ksend, kbuf.at[i], kv_devs[i]))
-        q_cps[off] = send(qsend, qbuf.at[off], y_to[off])
-    for i in range(7):
-        v_cps.append(send(vsend, vbuf.at[i], kv_devs[i]))
+    kvsend[0] = jnp.where(left, kk[:DH], kk[DH:])
+    kvsend[1] = qkv[DH : 2 * DH]
+
+    q_cps, kv_cps = {}, {}
+
+    def send_kv(*slots):
+        for i in slots:
+            kv_cps[i] = send(kvsend, kvbuf.at[i - 1], kv_devs[i - 1])
+
+    def send_q(*slots):
+        for off in slots:
+            q_cps[off] = send(qsend, qbuf.at[off], y_to[off])
+
+    for i, off in zip(KV_SENDS, Q_SENDS):
+        send_kv(i)
+        send_q(off)
+    fence()
 
     for cp in w_x:
         cp.wait_recv()
@@ -211,15 +233,6 @@
         fot[z] = stacked(fo[:, z * 128 : (z + 1) * 128].T)
         n1g[pl.ds(z * 128, 128), :] = column(vec[1, z : z + 1, :])
         n1b[pl.ds(z * 128, 128), :] = column(vec[2, z : z + 1, :])
-    w_c.wait_recv()
-    for z in range(NZH):
-        block = jnp.concatenate(
-            [gath[par, xx, z] for par in range(NC) for xx in range(NX)], axis=0
-        )
-        top, rest = halves(block.T)
-        wot[:D, z * 128 : (z + 1) * 128] = top
-        wot[D:, z * 128 : (z + 1) * 128] = rest
-
     def put_key(i, pack):
         other = pltpu.roll(pack, DH, 1)
         for j, kd in enumerate((jnp.where(left, pack, other), jnp.where(left, other, pack))):
@@ -238,23 +251,22 @@
     def put_value(i, vt):
         vst[:, i * ROWS : (i + 1) * ROWS] = stacked(vt)
 
-    put_key(7, ksend[...])
-    put_value(7, vsend[...])
-    put_query(7, qsend[...])
-    for i in range(7):
-        k_cps[i].wait_recv()
-        put_key(i, kbuf[i])
-    for i in range(7):
-        v_cps[i].wait_recv()
-        put_value(i, vbuf[i])
+    def put_kv(i):
+        kv = kvbuf.at[i - 1] if i else kvsend
+        put_key(i, kv[0])
+        put_value(i, kv[1])
+
+    put_kv(0)
+    put_query(0, qsend[...])
+    places = {off: 2 * pair + j for pair in range(4) for j, off in enumerate(Q_PAIRS[pair])}
+    for i, off in zip(KV_SENDS, Q_SENDS):
+        kv_cps[i].wait_recv()
+        put_kv(i)
+        q_cps[off].wait_recv()
+        put_query(places[off], qbuf[off])
 
     o_cps = {}
-    for pair in range(4):
-        for j in (2 * pair, 2 * pair + 1):
-            off = Y_ORDER[j]
-            if off:
-                q_cps[off].wait_recv()
-                put_query(j, qbuf[off])
+    for pair in (3, 2, 1, 0):
         s = mxu(kst[...], qst[:, 2 * pair * ROWS : (2 * pair + 2) * ROWS])
         top_score = jnp.max(s, axis=0, keepdims=True)
         p = jnp.exp2(s - top_score)
@@ -262,9 +274,9 @@
         p_top, p_rest = halves(p)
         o = mxu(vst[...], p_top) + mxu(vst[...], p_rest)
         o = o[:DH] + o[DH:]
-        for j in (2 * pair, 2 * pair + 1):
-            off = Y_ORDER[j]
-            cols = slice((j % 2) * ROWS, (j % 2 + 1) * ROWS)
+        for j in (1, 0):
+            off = Q_PAIRS[pair][j]
+            cols = slice(j * ROWS, (j + 1) * ROWS)
             osend[off, :DH] = o[:, cols]
             osend[off, DH : DH + 8] = jnp.concatenate(
                 [
@@ -275,6 +287,18 @@
             )
             if off:
                 o_cps[off] = send(osend.at[off], obuf.at[off], y_from[off])
+        if pair:
+            fence()
+
+    w_c.wait_recv()
+    for z in range(NZH):
+        block = jnp.concatenate(
+            [gath[par, xx, z] for par in range(NC) for xx in range(NX)], axis=0
+        )
+        top, rest = halves(block.T)
+        wot[:D, z * 128 : (z + 1) * 128] = top
+        wot[D:, z * 128 : (z + 1) * 128] = rest
+
 
     for off in range(1, NY):
         o_cps[off].wait_recv()
@@ -305,15 +329,16 @@
     for k in range(4):
         fpart[k] = quads(mxu(fot[z_order[k]], hid2), 128, ROWS).reshape(NC, DH, ROWS)
         fcore.append(send(fpart.at[k, oc], fcbuf.at[k], core_dev))
+        fence()
     fz = []
     for k in range(4):
         fcore[k].wait_recv()
-        fsbuf[k] = fpart[k, c] + fcbuf[k]
-        if k < 3:
-            fz.append(send(fsbuf.at[k], frsbuf.at[k], z_devs[k]))
+        chip_sum = fpart[k, c] + fcbuf[k]
+        fsbuf[k] = chip_sum + normed_ref[h] if k == 2 else chip_sum
+        fz.append(send(fsbuf.at[k], frsbuf.at[k], sum_devs[k]))
     for cp in fz:
         cp.wait_recv()
-    r2 = (fsbuf[3] + frsbuf[1]) + (frsbuf[0] + frsbuf[2]) + normed_ref[h]
+    r2 = (frsbuf[0] + frsbuf[1]) + (frsbuf[2] + frsbuf[3])
 
     mean_own = jnp.sum(r2, axis=0, keepdims=True) * (1.0 / DH)
     dev_own = r2 - mean_own
@@ -340,18 +365,18 @@
     vb = lambda *shape: pltpu.VMEM(shape, BF16)
     block = (DH, ROWS)
     scratch = [
-        vm(ROWS, 1024), vm(4, 1024, 128), vm(D, DH), vm(D, DH), vm(D, DH), vm(DH, D),
+        vm(ROWS, 1024), vm(4, 1024, 128), vm(DH, D), vm(DH, D), vm(DH, D), vm(DH, D),
         vm(D, FF_PART), vm(FF_PART, D), vm(5, 4, 128),
         vb(8 * DH, D), vb(2 * FF_PART, D), vb(4, 256, FF_PART), vb(2 * D, D),
         vm(NC, NX, NZH, 16, D), vm(D, ROWS), vm(D, ROWS), vm(3, NC, *block),
-        vm(4, NC, *block), vm(4, *block), vm(4, *block), vm(3, *block), vm(NHEAD, *block),
-        vm(*block), vm(*block), vm(*block), vm(NY, *block), vm(7, *block), vm(7, *block),
+        vm(4, NC, *block), vm(4, *block), vm(4, *block), vm(4, *block), vm(NHEAD, *block),
+        vm(*block), vm(2, *block), vm(NY, *block), vm(7, 2, *block),
         vb(1024, 256), vb(256, 1024), vb(128, 1024),
         vm(NY, DH + 8, ROWS), vm(NY, DH + 8, ROWS), vm(NHEAD, *block), vm(NHEAD, *block),
-        vm(4, NC, *block), vm(4, *block), vm(4, *block), vm(3, *block),
+        vm(4, NC, *block), vm(4, *block), vm(4, *block), vm(4, *block),
         vm(8, ROWS), vm(7, 8, ROWS),
         pltpu.SemaphoreType.DMA((16,)), pltpu.SemaphoreType.DMA((COPIES,)),
-        pltpu.SemaphoreType.DMA((COPIES,)),
+        pltpu.SemaphoreType.DMA((COPIES,)), pltpu.SemaphoreType.REGULAR,
     ]
     return pl.pallas_call(
         layer_kernel,
@@ -360,10 +385,10 @@
         out_specs=pl.BlockSpec(memory_space=pltpu.VMEM),
         scratch_shapes=scratch,
         compiler_params=pltpu.CompilerParams(
-            collective_id=0, has_side_effects=True, vmem_limit_bytes=40 * 1024 * 1024
+            collective_id=0, has_side_effects=True, vmem_limit_bytes=60 * 1024 * 1024
         ),
         name="layer",
-    )(series, emb_weight, vec4(emb_bias), q_weight, k_weight, v_weight, out_weight,
+    )(series, emb_weight, vec4(emb_bias), q_weight.T, k_weight.T, v_weight.T, out_weight,
       vec4(norm1_gain), vec4(norm1_bias), ffn_in, ffn_out, vec4(norm2_gain), vec4(norm2_bias))
 
 

time: 84.1 us -> 71.5 us (0.85)
  local copies, waits for them, and re-layouts: 12.7 us -> 1.38 us
  Pallas kernels: 70.9 us -> 69.9 us
    unnamed x24 -> x1, local copies, waits for them, and re-layouts: 12.7 us -> 1.38 us
    pallas_call x1, Pallas kernels: 70.9 us -> 69.9 us  [on_device(): pl.pallas_call(layer_kernel, out_shape=jax.ShapeDtypeStruct(block, F32),...]
where the time goes in v2:
time: 71.5 us; the launch traced here: 71.3 us
  Pallas kernels  69.9 us (98%)
  local copies, waits for them, and re-layouts  1.38 us (2%)
    pallas_call x1, Pallas kernels, on_device(): pl.pallas_call(layer_kernel, out_shape=jax.ShapeDtypeStruct(block, F32),...  69.9 us

profile of v2, /device:TPU:1, one launch (start us, length us, event | category | flops | bytes accessed | tf_op | source)
XLA Modules:
  0.0 71.3 jit_solution(17399738448990588742)
XLA Ops:
  0.0 69.9 %layer.1 = f32[64,128]{1,0:T(8,128)} custom-call(f32[128,1024]{1,0:T(8,128)} %series_h.1, f32[1024,512]{1,0:T(8,128)} %ew_h.1, f32[4,128]{1,0:T(4,128)} %bitcast.11, f32[64,512]{1,0:T(8,128)} %bitcast.8, f32[64,512]{1,0:T(8,128)} %bitcast.9, f32[64,512]{1,0:T(8,128)} %bitcast.10, f32[64,512]{1,0:T(8,128)} %ow_h.1, f32[4,128]{1,0:T(4,128)} %bitcast.12, ...), custom_call_target="tpu_custom_call" | custom-call | tf_op jit(solution)/shard_map/layer/pallas_call | solution.py:381
  69.9 1.4 %copy.15 = f32[64,128]{1,0:T(8,128)} copy(f32[64,128]{1,0:T(8,128)} %layer.1) | data formatting | bytes 65536

commit v3 on v2

--- a/solution.py
+++ b/solution.py
@@ -78,7 +78,6 @@
     z_order = [(zh + off) % NZH for off in sum_offs]
     sum_devs = [at(y, x, 1 - zl, zz, c) for zz in z_order]
     x_devs = [at(y, (x + off) % NX, zl, zh, c) for off in (2, 1, 3)]
-    head_devs = [(v, (h + off) % NHEAD) for off in (4, 3, 5, 2, 6, 7, 1)]
     y_to = {off: at((y + off) % NY, x, zl, zh, c) for off in range(1, NY)}
     y_from = {off: at((y + NY - off) % NY, x, zl, zh, c) for off in range(1, NY)}
     kv_devs = [at(y, (x + dx) % NX, (zl + dz) % NZL, zh, c) for dx, dz in KV_OFFS]
@@ -97,8 +96,8 @@
         pending.append(cp)
         return cp
 
-    def drain():
-        while pending:
+    def drain(keep=0):
+        while len(pending) > keep:
             pending.pop(0).wait_send()
 
     def fence():
@@ -115,29 +114,31 @@
         return cp
 
     ld_series = load(series_h, series)
-    ld_ew = [
-        load(ew_h.at[:, pl.ds(pl.multiple_of(zz * 128, 128), 128)], ew.at[k])
-        for k, zz in enumerate(z_order)
-    ]
+
+    def load_ew(k):
+        cols = pl.ds(pl.multiple_of(z_order[k] * 128, 128), 128)
+        return load(ew_h.at[:, cols], ew.at[k])
+
+    ld_ew = [load_ew(0)]
     barrier = pltpu.get_barrier_semaphore()
-    greeted = head_devs + sum_devs[:2] + sum_devs[3:] + [y_to[off] for off in range(1, NY)] + kv_devs
+    greeted = z_devs + [core_dev] + sum_devs[:2] + sum_devs[3:] + [y_to[off] for off in range(1, NY)] + kv_devs
     for dev in greeted:
         pl.semaphore_signal(barrier, inc=1, device_id=dev, device_id_type=MESH)
+    ld_ew += [load_ew(k) for k in (1, 2, 3)]
+
+    ld_series.wait()
+    s_stack = stacked(series[...])
+
+    def emb_step(k):
+        ld_ew[k].wait()
+        r = mxu(s_stack, side_by_side(ew[k]))
+        epart[k] = quads(r, ROWS, 128).T.reshape(NC, DH, ROWS)
+
+    emb_step(0)
     ld_ow = load(ow_h, ow)
     ld_vec = [load(r, vec.at[i]) for i, r in enumerate((eb_h, n1g_h, n1b_h, n2g_h, n2b_h))]
     ld_qkv = [load(a, b) for a, b in ((qw_h, qw), (kw_h, kw), (vw_h, vw))]
     ld_ffn = [load(a, b) for a, b in ((fi_h, fi), (fo_h, fo))]
-
-    ld_series.wait()
-    s_stack = stacked(series[...])
-
-    def emb_step(k):
-        ld_ew[k].wait()
-        r = mxu(s_stack, side_by_side(ew[k]))
-        epart[k] = quads(r, ROWS, 128).T.reshape(NC, DH, ROWS)
-
-    emb_step(0)
-    ld_ow.wait()
     pl.semaphore_wait(barrier, len(greeted))
 
     core_cps = [send(epart.at[0, oc], cbuf.at[0], core_dev)]
@@ -163,6 +164,7 @@
     to_chip(2)
     to_chip(3)
 
+    ld_ow.wait()
     xrows = pl.ds(pl.multiple_of(x * 16, 16), 16)
     gath[c, x, zh] = ow[xrows, :]
     w_z = [send(gath.at[c, x, zh], gath.at[c, x, zh], dev) for dev in z_devs]
@@ -183,6 +185,7 @@
         zs = [send(buf.at[h], buf.at[h], dev) for dev in z_devs]
         cs = [send(buf.at[h], buf.at[h], core_dev)]
         fence()
+        drain(keep=4)
         meanwhile()
         for k in (1, 2, 0):
             zs[k].wait_recv()
@@ -191,12 +194,9 @@
         for cp in cs:
             cp.wait_recv()
 
-    w_x = []
-
     def prepare_ffn_in():
         for cp in w_z:
             cp.wait_recv()
-        w_x.extend(send(gath.at[c, x], gath.at[c, x], dev) for dev in x_devs)
         ld_ffn[0].wait()
         fit[...] = stacked(fi[...].T)
 
@@ -224,10 +224,8 @@
         send_kv(i)
         send_q(off)
     fence()
-
-    for cp in w_x:
-        cp.wait_recv()
-    w_c = send(gath.at[c], gath.at[c], core_dev)
+    drain(keep=14)
+
     ld_ffn[1].wait()
     for z in range(NZH):
         fot[z] = stacked(fo[:, z * 128 : (z + 1) * 128].T)
@@ -278,41 +276,41 @@
             off = Q_PAIRS[pair][j]
             cols = slice(j * ROWS, (j + 1) * ROWS)
             osend[off, :DH] = o[:, cols]
-            osend[off, DH : DH + 8] = jnp.concatenate(
-                [
-                    jnp.broadcast_to(top_score[:, cols], (4, ROWS)),
-                    jnp.broadcast_to(total[:, cols], (4, ROWS)),
-                ],
-                axis=0,
-            )
+            osend[off, DH : DH + 1] = top_score[:, cols]
+            osend[off, DH + 1 : DH + 2] = total[:, cols]
             if off:
                 o_cps[off] = send(osend.at[off], obuf.at[off], y_from[off])
         if pair:
             fence()
 
-    w_c.wait_recv()
-    for z in range(NZH):
-        block = jnp.concatenate(
-            [gath[par, xx, z] for par in range(NC) for xx in range(NX)], axis=0
-        )
-        top, rest = halves(block.T)
-        wot[:D, z * 128 : (z + 1) * 128] = top
-        wot[D:, z * 128 : (z + 1) * 128] = rest
-
+    w_x = [send(gath.at[c, x], gath.at[c, x], dev) for dev in x_devs]
+    drain(keep=10)
+
+    def prepare_out_weight():
+        for cp in w_x:
+            cp.wait_recv()
+        send(gath.at[c], gath.at[c], core_dev).wait_recv()
+        for z in range(NZH):
+            block = jnp.concatenate(
+                [gath[par, xx, z] for par in range(NC) for xx in range(NX)], axis=0
+            )
+            top, rest = halves(block.T)
+            wot[:D, z * 128 : (z + 1) * 128] = top
+            wot[D:, z * 128 : (z + 1) * 128] = rest
 
     for off in range(1, NY):
         o_cps[off].wait_recv()
     tops = [osend[0, DH : DH + 1]] + [obuf[off, DH : DH + 1] for off in range(1, NY)]
     best = functools.reduce(jnp.maximum, tops)
     scales = [jnp.exp2(t - best) for t in tops]
-    denom = scales[0] * osend[0, DH + 4 : DH + 5]
+    denom = scales[0] * osend[0, DH + 1 : DH + 2]
     acc = scales[0] * osend[0, :DH]
     for off in range(1, NY):
-        denom += scales[off] * obuf[off, DH + 4 : DH + 5]
+        denom += scales[off] * obuf[off, DH + 1 : DH + 2]
         acc += scales[off] * obuf[off, :DH]
     mfull[h] = acc / denom
 
-    gather_heads(mfull, lambda: None)
+    gather_heads(mfull, prepare_out_weight)
 
     mixed_t = mfull[...].reshape(D, ROWS)
     resid = emb_t + quads(mxu(wot[...], side_by_side(mixed_t)), D, ROWS)
@@ -336,6 +334,7 @@
         chip_sum = fpart[k, c] + fcbuf[k]
         fsbuf[k] = chip_sum + normed_ref[h] if k == 2 else chip_sum
         fz.append(send(fsbuf.at[k], frsbuf.at[k], sum_devs[k]))
+    drain(keep=8)
     for cp in fz:
         cp.wait_recv()
     r2 = (frsbuf[0] + frsbuf[1]) + (frsbuf[2] + frsbuf[3])
@@ -343,16 +342,22 @@
     mean_own = jnp.sum(r2, axis=0, keepdims=True) * (1.0 / DH)
     dev_own = r2 - mean_own
     m2_own = jnp.sum(dev_own * dev_own, axis=0, keepdims=True)
-    stat[...] = jnp.concatenate(
-        [jnp.broadcast_to(mean_own, (4, ROWS)), jnp.broadcast_to(m2_own, (4, ROWS))], axis=0
-    )
-    st = [send(stat, statbuf.at[i], dev) for i, dev in enumerate(head_devs)]
+    stat[0, 0:1] = mean_own
+    stat[0, 1:2] = m2_own
+    send(stat.at[0], statbuf.at[3], core_dev).wait_recv()
+    gap = mean_own - statbuf[3, 0:1]
+    mean_pair = 0.5 * (mean_own + statbuf[3, 0:1])
+    m2_pair = m2_own + statbuf[3, 1:2] + (0.5 * DH) * gap * gap
+    stat[1, 0:1] = mean_pair
+    stat[1, 1:2] = m2_pair
+    st = [send(stat.at[1], statbuf.at[i], dev) for i, dev in enumerate(z_devs)]
+    drain(keep=3)
     for cp in st:
         cp.wait_recv()
-    means = [mean_own] + [statbuf[i, 0:1] for i in range(7)]
-    mean = functools.reduce(jnp.add, means) * (1.0 / NHEAD)
-    m2 = functools.reduce(jnp.add, [m2_own] + [statbuf[i, 4:5] for i in range(7)])
-    m2 += DH * functools.reduce(jnp.add, [(m - mean) * (m - mean) for m in means])
+    means = [mean_pair] + [statbuf[i, 0:1] for i in range(3)]
+    mean = functools.reduce(jnp.add, means) * (1.0 / NZH)
+    m2 = functools.reduce(jnp.add, [m2_pair] + [statbuf[i, 1:2] for i in range(3)])
+    m2 += 2 * DH * functools.reduce(jnp.add, [(m - mean) * (m - mean) for m in means])
     scale = lax.rsqrt(m2 * (1.0 / D) + EPS)
     out_ref[...] = (r2 - mean) * scale * own_vec[1, c] + own_vec[2, c]
     drain()
@@ -372,9 +377,9 @@
         vm(4, NC, *block), vm(4, *block), vm(4, *block), vm(4, *block), vm(NHEAD, *block),
         vm(*block), vm(2, *block), vm(NY, *block), vm(7, 2, *block),
         vb(1024, 256), vb(256, 1024), vb(128, 1024),
-        vm(NY, DH + 8, ROWS), vm(NY, DH + 8, ROWS), vm(NHEAD, *block), vm(NHEAD, *block),
+        vm(NY, DH + 2, ROWS), vm(NY, DH + 2, ROWS), vm(NHEAD, *block), vm(NHEAD, *block),
         vm(4, NC, *block), vm(4, *block), vm(4, *block), vm(4, *block),
-        vm(8, ROWS), vm(7, 8, ROWS),
+        vm(2, 2, ROWS), vm(4, 2, ROWS),
         pltpu.SemaphoreType.DMA((16,)), pltpu.SemaphoreType.DMA((COPIES,)),
         pltpu.SemaphoreType.DMA((COPIES,)), pltpu.SemaphoreType.REGULAR,
     ]

time: 71.5 us -> 69.9 us (0.978)
  Pallas kernels: 69.9 us -> 68.4 us
    pallas_call x1, Pallas kernels: 69.9 us -> 68.4 us  [on_device(): pl.pallas_call(layer_kernel, out_shape=jax.ShapeDtypeStruct(block, F32),...]
where the time goes in v3:
time: 69.9 us; the launch traced here: 69.7 us
  Pallas kernels  68.4 us (98%)
  local copies, waits for them, and re-layouts  1.38 us (2%)
    pallas_call x1, Pallas kernels, on_device(): pl.pallas_call(layer_kernel, out_shape=jax.ShapeDtypeStruct(block, F32),...  68.4 us

profile of v3, /device:TPU:1, one launch (start us, length us, event | category | flops | bytes accessed | tf_op | source)
XLA Modules:
  0.0 69.7 jit_solution(1724583645370144512)
XLA Ops:
  0.0 68.4 %layer.1 = f32[64,128]{1,0:T(8,128)} custom-call(f32[128,1024]{1,0:T(8,128)} %series_h.1, f32[1024,512]{1,0:T(8,128)} %ew_h.1, f32[4,128]{1,0:T(4,128)} %bitcast.11, f32[64,512]{1,0:T(8,128)} %bitcast.8, f32[64,512]{1,0:T(8,128)} %bitcast.9, f32[64,512]{1,0:T(8,128)} %bitcast.10, f32[64,512]{1,0:T(8,128)} %ow_h.1, f32[4,128]{1,0:T(4,128)} %bitcast.12, ...), custom_call_target="tpu_custom_call" | custom-call | tf_op jit(solution)/shard_map/layer/pallas_call | solution.py:386
  68.4 1.4 %copy.15 = f32[64,128]{1,0:T(8,128)} copy(f32[64,128]{1,0:T(8,128)} %layer.1) | data formatting | bytes 65536

commit v4 on v3

--- a/solution.py
+++ b/solution.py
@@ -284,12 +284,16 @@
             fence()
 
     w_x = [send(gath.at[c, x], gath.at[c, x], dev) for dev in x_devs]
-    drain(keep=10)
+    w_c = [send(gath.at[c, x], gath.at[c, x], core_dev)]
+    drain(keep=11)
 
     def prepare_out_weight():
-        for cp in w_x:
+        for k, off in ((1, 1), (2, 3), (0, 2)):
+            w_x[k].wait_recv()
+            xs = (x + NX - off) % NX
+            w_c.append(send(gath.at[c, xs], gath.at[c, xs], core_dev))
+        for cp in w_c:
             cp.wait_recv()
-        send(gath.at[c], gath.at[c], core_dev).wait_recv()
         for z in range(NZH):
             block = jnp.concatenate(
                 [gath[par, xx, z] for par in range(NC) for xx in range(NX)], axis=0

time: 69.9 us -> 70 us (level)
  no operation moved by 1% of the time
where the time goes in v4:
time: 70 us; the launch traced here: 69.8 us
  Pallas kernels  68.4 us (98%)
  local copies, waits for them, and re-layouts  1.38 us (2%)
    pallas_call x1, Pallas kernels, on_device(): pl.pallas_call(layer_kernel, out_shape=jax.ShapeDtypeStruct(block, F32),...  68.4 us

profile of v4, /device:TPU:1, one launch (start us, length us, event | category | flops | bytes accessed | tf_op | source)
XLA Modules:
  0.0 69.8 jit_solution(2773370227138821139)
XLA Ops:
  0.0 68.4 %layer.1 = f32[64,128]{1,0:T(8,128)} custom-call(f32[128,1024]{1,0:T(8,128)} %series_h.1, f32[1024,512]{1,0:T(8,128)} %ew_h.1, f32[4,128]{1,0:T(4,128)} %bitcast.11, f32[64,512]{1,0:T(8,128)} %bitcast.8, f32[64,512]{1,0:T(8,128)} %bitcast.9, f32[64,512]{1,0:T(8,128)} %bitcast.10, f32[64,512]{1,0:T(8,128)} %ow_h.1, f32[4,128]{1,0:T(4,128)} %bitcast.12, ...), custom_call_target="tpu_custom_call" | custom-call | tf_op jit(solution)/shard_map/layer/pallas_call | solution.py:390
  68.4 1.4 %copy.15 = f32[64,128]{1,0:T(8,128)} copy(f32[64,128]{1,0:T(8,128)} %layer.1) | data formatting | bytes 65536

commit v5 on v3

--- a/solution.py
+++ b/solution.py
@@ -57,9 +57,9 @@
     out_ref,
     series, ew, qw, kw, vw, ow, fi, fo, vec,
     wqkv, fit, fot, wot, gath, n1g, n1b, own_vec,
-    epart, cbuf, sbuf, rsbuf, efull,
+    epart, cbuf, sbuf, rsbuf, eown, efull, e2full,
     qsend, kvsend, qbuf, kvbuf, kst, qst, vst,
-    osend, obuf, mfull, normed_ref,
+    osend, obuf, mown, mfull, normed_ref,
     fpart, fcbuf, fsbuf, frsbuf, stat, statbuf,
     lsem, ssem, rsem, own_sem,
 ):
@@ -179,19 +179,26 @@
 
     for cp in z_cps:
         cp.wait_recv()
-    efull[h] = (rsbuf[0] + rsbuf[1]) + (rsbuf[2] + rsbuf[3]) + own_vec[0, c]
-
-    def gather_heads(buf, meanwhile):
-        zs = [send(buf.at[h], buf.at[h], dev) for dev in z_devs]
-        cs = [send(buf.at[h], buf.at[h], core_dev)]
+    eown[...] = (rsbuf[0] + rsbuf[1]) + (rsbuf[2] + rsbuf[3]) + own_vec[0, c]
+
+    def start_gather(block, full):
+        return [send(block, full.at[h], dev) for dev in sum_devs]
+
+    def share_gather(zs, full):
+        cs = []
+        for k in (2, 3, 1, 0):
+            zs[k].wait_recv()
+            off = (2, 3 - 2 * zl, 0, 1 + 2 * zl)[k]
+            hs = ((zh + NZH - off) % NZH) * NC + c
+            cs.append(send(full.at[hs], full.at[hs], core_dev))
+        return cs
+
+    def gather_heads(block, full, meanwhile):
+        zs = start_gather(block, full)
         fence()
         drain(keep=4)
         meanwhile()
-        for k in (1, 2, 0):
-            zs[k].wait_recv()
-            hs = ((zh + NZH - Z_OFFS[k]) % NZH) * NC + c
-            cs.append(send(buf.at[hs], buf.at[hs], core_dev))
-        for cp in cs:
+        for cp in share_gather(zs, full):
             cp.wait_recv()
 
     def prepare_ffn_in():
@@ -200,7 +207,7 @@
         ld_ffn[0].wait()
         fit[...] = stacked(fi[...].T)
 
-    gather_heads(efull, prepare_ffn_in)
+    gather_heads(eown, efull, prepare_ffn_in)
 
     emb_t = efull[...].reshape(D, ROWS)
     qkv = quads(mxu(wqkv[...], side_by_side(emb_t)), 4 * DH, ROWS)
@@ -284,7 +291,8 @@
             fence()
 
     w_x = [send(gath.at[c, x], gath.at[c, x], dev) for dev in x_devs]
-    drain(keep=10)
+    e_cps = start_gather(efull.at[h], e2full)
+    drain(keep=14)
 
     def prepare_out_weight():
         for cp in w_x:
@@ -298,6 +306,8 @@
             wot[:D, z * 128 : (z + 1) * 128] = top
             wot[D:, z * 128 : (z + 1) * 128] = rest
 
+    e_shared = share_gather(e_cps, e2full)
+
     for off in range(1, NY):
         o_cps[off].wait_recv()
     tops = [osend[0, DH : DH + 1]] + [obuf[off, DH : DH + 1] for off in range(1, NY)]
@@ -308,12 +318,14 @@
     for off in range(1, NY):
         denom += scales[off] * obuf[off, DH + 1 : DH + 2]
         acc += scales[off] * obuf[off, :DH]
-    mfull[h] = acc / denom
-
-    gather_heads(mfull, prepare_out_weight)
+    mown[...] = acc / denom
+
+    gather_heads(mown, mfull, prepare_out_weight)
+    for cp in e_shared:
+        cp.wait_recv()
 
     mixed_t = mfull[...].reshape(D, ROWS)
-    resid = emb_t + quads(mxu(wot[...], side_by_side(mixed_t)), D, ROWS)
+    resid = e2full[...].reshape(D, ROWS) + quads(mxu(wot[...], side_by_side(mixed_t)), D, ROWS)
     centre = jnp.sum(resid, axis=0, keepdims=True) * (1.0 / D)
     spread = resid - centre
     variance = jnp.sum(spread * spread, axis=0, keepdims=True) * (1.0 / D)
@@ -374,10 +386,11 @@
         vm(D, FF_PART), vm(FF_PART, D), vm(5, 4, 128),
         vb(8 * DH, D), vb(2 * FF_PART, D), vb(4, 256, FF_PART), vb(2 * D, D),
         vm(NC, NX, NZH, 16, D), vm(D, ROWS), vm(D, ROWS), vm(3, NC, *block),
-        vm(4, NC, *block), vm(4, *block), vm(4, *block), vm(4, *block), vm(NHEAD, *block),
+        vm(4, NC, *block), vm(4, *block), vm(4, *block), vm(4, *block), vm(*block),
+        vm(NHEAD, *block), vm(NHEAD, *block),
         vm(*block), vm(2, *block), vm(NY, *block), vm(7, 2, *block),
         vb(1024, 256), vb(256, 1024), vb(128, 1024),
-        vm(NY, DH + 2, ROWS), vm(NY, DH + 2, ROWS), vm(NHEAD, *block), vm(NHEAD, *block),
+        vm(NY, DH + 2, ROWS), vm(NY, DH + 2, ROWS), vm(*block), vm(NHEAD, *block), vm(NHEAD, *block),
         vm(4, NC, *block), vm(4, *block), vm(4, *block), vm(4, *block),
         vm(2, 2, ROWS), vm(4, 2, ROWS),
         pltpu.SemaphoreType.DMA((16,)), pltpu.SemaphoreType.DMA((COPIES,)),

time: 69.9 us -> 70.1 us (level)
  no operation moved by 1% of the time
where the time goes in v5:
time: 70.1 us; the launch traced here: 69.9 us
  Pallas kernels  68.5 us (98%)
  local copies, waits for them, and re-layouts  1.38 us (2%)
    pallas_call x1, Pallas kernels, on_device(): pl.pallas_call(layer_kernel, out_shape=jax.ShapeDtypeStruct(block, F32),...  68.5 us

profile of v5, /device:TPU:1, one launch (start us, length us, event | category | flops | bytes accessed | tf_op | source)
XLA Modules:
  0.0 69.9 jit_solution(8606545002012223444)
XLA Ops:
  0.0 68.5 %layer.1 = f32[64,128]{1,0:T(8,128)} custom-call(f32[128,1024]{1,0:T(8,128)} %series_h.1, f32[1024,512]{1,0:T(8,128)} %ew_h.1, f32[4,128]{1,0:T(4,128)} %bitcast.11, f32[64,512]{1,0:T(8,128)} %bitcast.8, f32[64,512]{1,0:T(8,128)} %bitcast.9, f32[64,512]{1,0:T(8,128)} %bitcast.10, f32[64,512]{1,0:T(8,128)} %ow_h.1, f32[4,128]{1,0:T(4,128)} %bitcast.12, ...), custom_call_target="tpu_custom_call" | custom-call | tf_op jit(solution)/shard_map/layer/pallas_call | solution.py:399
  68.5 1.4 %copy.15 = f32[64,128]{1,0:T(8,128)} copy(f32[64,128]{1,0:T(8,128)} %layer.1) | data formatting | bytes 65536
